TPU v7x, 32 devices: a whole 2x2x4 slice. The times are simulated.
32 devices in a mesh: rep: 2 (over x), dp: 8 (over z, y), tensor: 2 (over core).
Axes of the slice: x: 2, y: 2, z: 4, core: 2. Of those that a mesh axis runs over, the one named last changes fastest.
Arguments:
- rubric_query: bfloat16 [64, 256, 4096], P(('rep', 'dp'), None, 'tensor'), parts along dimension 0, may hold values from -48 to 48
- rubric_key: bfloat16 [64, 256, 512], P(('rep', 'dp'), None, 'tensor'), parts along dimension 0, may hold values from -4 to 4
- rubric_value: bfloat16 [64, 256, 512], P(('rep', 'dp'), None, 'tensor'), parts along dimension 0, may hold values from -6 to 6
- response_states: bfloat16 [64, 256, 8192], P(('rep', 'dp'), None, 'tensor'), parts along dimension 0, may hold values from -6 to 6
- key_weight: bfloat16 [8192, 512], P('tensor'), may hold values from -0.0625 to 0.0625
- value_weight: bfloat16 [8192, 512], P('tensor'), may hold values from -0.0625 to 0.0625
- owner_slot: int32 [64], P('rep'), parts along dimension 0, may hold values from 0 to 31, as said below
- response_length: int32 [64], P('rep'), parts along dimension 0, may hold values from 128 to 256, as said below
- pair_table: int32 [64, 2], P('rep'), parts along dimension 0, may hold values from 0 to 31, as said below
Outputs:
- judge_context: bfloat16 [64, 256, 4096], P(('rep', 'dp'), None, 'tensor'), parts along dimension 0
There are 2 independent parts, one for each index of `rep`. A program takes and returns all parts, laid end to end along the dimension named above; an argument that names none is the same for every part. Nothing has to cross between parts.
Inputs may be any that keep to these rules, and one draw needn't show every extreme that they name: A permutation: response r is stored in row owner_slot[r] of response_states, on index owner_slot[r] // 4 of dp. `response_length`: indexed by response; rows past a response's length are padding; some response has exactly 256 tokens. `pair_table`: rows 4 * g to 4 * g + 3 are the pair tasks of index g of dp; the 8 responses named in them are distinct and stored on 8 distinct indices of dp.
All inputs are finite; a program needn't handle non-finite values.
Results may differ from a plain program's by a relative error of at most 0.008.
Values may be sent and summed in bfloat16 or wider, within the bound.
No kernel may reach another device: no remote copies, remote signals or barrier semaphores. Data moves between devices by JAX's collectives and lax.ppermute only.
A program may use at most 192 MiB of HBM per device.

v0:
```python
import functools
import math

import jax
import jax.numpy as jnp
from jax import lax
from jax.experimental import pallas as pl
from jax.experimental.pallas import tpu as pltpu
from jax.sharding import PartitionSpec as P

HD = 128
SCALE = HD ** (-0.5) * math.log2(math.e)
MIB = 1024 * 1024
FIELDS = 5
NEVER = -1e30
NEAR = 100.0
FAR = 1e30
TOGETHER = 2
EXTRA_ROWS = 16
SHIFT_ROW = HD + EXTRA_ROWS // 2
ANY = pl.BlockSpec(memory_space=pl.ANY)
SMEM = pl.BlockSpec(memory_space=pltpu.SMEM)
WHOLE = pl.BlockSpec(memory_space=pltpu.VMEM)


def params(*semantics, vmem=12):
    return pltpu.CompilerParams(
        dimension_semantics=semantics or None, vmem_limit_bytes=vmem * MIB
    )


def hint(flops, bytes_accessed, transcendentals):
    return pl.CostEstimate(
        flops=flops, bytes_accessed=bytes_accessed, transcendentals=transcendentals
    )


def arrival_order(groups):
    far = list(range(groups - 1, groups // 2 - 1, -1))
    near = list(range(groups // 2 - 1, 0, -1))
    order = []
    for at in range(len(far)):
        order += far[at : at + 1] + near[at : at + 1]
    return order


def write_plan(groups, stored, me, owner_ref, length_ref, table_ref, place_ref, plan_ref):
    pairs = table_ref.shape[1] // groups
    bits = stored.bit_length() - 1

    def slot_of(group, j):
        response = table_ref[j % 2, group * pairs + j // 2]
        slot = owner_ref[response]
        return response, lax.shift_right_logical(slot, bits), slot & (stored - 1)

    for shift in range(groups):
        plan_ref[shift * FIELDS + 3] = 0
        plan_ref[shift * FIELDS + 1] = 0
        row = jnp.int32(0)
        for j in range(2 * pairs):
            _, source, slot_row = slot_of(me ^ shift, j)
            row = jnp.where(source == me, slot_row, row)
        plan_ref[shift * FIELDS] = row
    sources = [slot_of(me, j) for j in range(2 * pairs)]
    for j, (response, source, _) in enumerate(sources):
        shift = source ^ me
        later = place_ref[shift] > place_ref[sources[j ^ 1][1] ^ me]
        plan_ref[shift * FIELDS + 1] = jnp.int32(j // 2)
        plan_ref[shift * FIELDS + 2] = length_ref[response]
        plan_ref[shift * FIELDS + 3] = jnp.int32(1)
        plan_ref[shift * FIELDS + 4] = later.astype(jnp.int32)


def plan_kernel(groups, stored, me_ref, owner_ref, length_ref, table_ref, place_ref, plan_ref):
    write_plan(groups, stored, me_ref[0], owner_ref, length_ref, table_ref, place_ref, plan_ref)


def make_plan(me, tables, groups, stored):
    return pl.pallas_call(
        functools.partial(plan_kernel, groups, stored),
        out_shape=jax.ShapeDtypeStruct((groups * FIELDS,), jnp.int32),
        in_specs=[SMEM] * 5,
        out_specs=SMEM,
        name="plan",
    )(me[None], *tables)


def finish_kernel(length, plan_ref, half_ref, own_keys_ref, own_values_ref, keys_ref, values_ref, *out_refs):
    width = keys_ref.shape[1]
    own_columns = pl.ds(pl.multiple_of(half_ref[0] * width, width), width)
    for shift, out_ref in enumerate(out_refs):
        start = pl.multiple_of(plan_ref[shift * FIELDS] * length, length)
        rows = pl.ds(start, length)
        for at, (own_ref, other_ref) in enumerate(
            ((own_keys_ref, keys_ref), (own_values_ref, values_ref))
        ):
            total = own_ref[rows, own_columns] + other_ref[rows, :]
            out_ref[at * length : (at + 1) * length, :] = total.astype(out_ref.dtype)


def finish(plan, half, own_keys, own_values, other_keys, other_values, groups, length):
    total, width = other_keys.shape
    return pl.pallas_call(
        functools.partial(finish_kernel, length),
        out_shape=[jax.ShapeDtypeStruct((2 * length, width), jnp.bfloat16)] * groups,
        in_specs=[SMEM] * 2 + [WHOLE] * 4,
        out_specs=[WHOLE] * groups,
        compiler_params=params(),
        cost_estimate=hint(
            2 * groups * length * width, 16 * total * width + 4 * groups * length * width, 0
        ),
        name="finish",
    )(plan, half[None], own_keys, own_values, other_keys, other_values)


def times(a, b):
    return jnp.dot(a, b, preferred_element_type=jnp.float32)


def head_columns(h):
    return slice(h * HD, (h + 1) * HD)


def turned_values(values):
    count = values.shape[0]
    row = lax.broadcasted_iota(jnp.int32, (EXTRA_ROWS, count), 0)
    ones = jnp.where(row < EXTRA_ROWS // 2, 1.0, 0.0)
    return jnp.concatenate([values.astype(jnp.float32).T, ones], axis=0)


def longest_of(keys):
    keys = keys.astype(jnp.float32)
    return jnp.sqrt(jnp.max(jnp.sum(keys * keys, axis=1, keepdims=True)))


def in_range(reach, keys):
    return jnp.max(reach) * longest_of(keys) < NEAR


def keep_shift(state, shift):
    row = lax.broadcasted_iota(jnp.int32, state.shape, 0)
    return jnp.where(row >= SHIFT_ROW, shift, state)


def rubric_kernel(q_ref, k_ref, v_ref, *refs):
    qt_ref, reach_ref, state_ref = refs[-3:]
    rows = q_ref.shape[1]
    heads = q_ref.shape[2] // HD
    keys = k_ref[0]
    values = turned_values(v_ref[0]).astype(jnp.bfloat16)
    shape = (keys.shape[0], rows)
    causal = lax.broadcasted_iota(jnp.int32, shape, 0) <= lax.broadcasted_iota(jnp.int32, shape, 1)
    allowed = jnp.where(causal, 1.0, 0.0).astype(jnp.bfloat16)
    allowed = jnp.concatenate([allowed] * TOGETHER, axis=1)
    reach = jnp.zeros((1, rows), jnp.float32)
    for h in range(heads):
        turned = q_ref[0, :, head_columns(h)].T
        qt_ref[0, 0, :, h * rows : (h + 1) * rows] = turned
        turned = turned.astype(jnp.float32)
        reach = jnp.maximum(reach, jnp.sum(turned * turned, axis=0, keepdims=True))
    reach = jnp.broadcast_to(jnp.sqrt(jnp.max(reach)) * SCALE, reach_ref.shape[2:])
    near = in_range(reach, keys)
    reach_ref[0, 0] = jnp.where(near, reach, FAR)

    def scores(h, some):
        return times(keys, qt_ref[0, 0, :, h * rows : (h + some) * rows])

    @pl.when(near)
    def _():
        later = scores(0, TOGETHER)
        for h in range(0, heads, TOGETHER):
            s = later
            if h + TOGETHER < heads:
                later = scores(h + TOGETHER, TOGETHER)
            weights = jnp.exp2(s * SCALE).astype(jnp.bfloat16) * allowed
            state_ref[0, 0, :, h * rows : (h + TOGETHER) * rows] = times(values, weights)

    @pl.when(jnp.logical_not(near))
    def _():
        for h in range(heads):
            s = jnp.where(causal, scores(h, 1), NEVER)
            peak = jnp.max(s, axis=0, keepdims=True)
            weights = jnp.exp2((s - peak) * SCALE).astype(jnp.bfloat16)
            state_ref[0, 0, :, h * rows : (h + 1) * rows] = keep_shift(times(values, weights), peak)


def state_shapes(pairs, kv_heads, stacked):
    return [
        jax.ShapeDtypeStruct((pairs, kv_heads, HD, stacked), jnp.bfloat16),
        jax.ShapeDtypeStruct((pairs, kv_heads, 8, HD), jnp.float32),
        jax.ShapeDtypeStruct((pairs, kv_heads, HD + EXTRA_ROWS, stacked), jnp.float32),
    ]


def rubric_attention(first, some, query, key, value, state, after):
    pairs, rows, width = query.shape
    steps = key.shape[2] // HD
    step_width = width // steps
    stacked = step_width // HD * rows
    count = key.shape[1]

    def across(size):
        return pl.BlockSpec((1, rows, size), lambda p, g: (first + p, 0, g))

    return pl.pallas_call(
        rubric_kernel,
        grid=(some, steps),
        in_specs=[across(step_width), across(HD), across(HD)] + [ANY] * (1 + len(state)),
        out_specs=[
            pl.BlockSpec((1, 1, size, width), lambda p, g: (first + p, g, 0, 0))
            for size, width in ((HD, stacked), (8, HD), (HD + EXTRA_ROWS, stacked))
        ],
        out_shape=state_shapes(pairs, steps, stacked),
        input_output_aliases={4 + i: i for i in range(len(state))},
        compiler_params=params("arbitrary", "arbitrary"),
        cost_estimate=hint(
            6 * some * width * rows * count,
            some * rows * width * 8,
            some * width // HD * rows * count,
        ),
        name="rubric_attention",
    )(query, key, value, after, *state)


def response_kernel(shift, plan_ref, kv_ref, qt_ref, reach_ref, state_ref, *refs):
    reach_out, state_out, out_ref = refs[-3:]
    rows = out_ref.shape[1]
    heads = out_ref.shape[2] // HD
    count = kv_ref.shape[0] // 2
    length = plan_ref[shift * FIELDS + 2]
    wanted = plan_ref[shift * FIELDS + 3] == 1
    completes = plan_ref[shift * FIELDS + 4] == 1

    def stack(h, some):
        return slice(h * rows, (h + some) * rows)

    @pl.when(wanted)
    def _():
        keys = kv_ref[:count, :]
        values = turned_values(kv_ref[count:, :])
        live = lax.broadcasted_iota(jnp.int32, values.shape, 1) < length
        values = jnp.where(live, values, 0.0).astype(jnp.bfloat16)
        near = in_range(reach_ref[...], keys)

        def scores(h, some):
            return times(keys, qt_ref[0, 0, :, stack(h, some)])

        @pl.when(near)
        def _():
            reach_out[...] = reach_ref[...]
            later = scores(0, TOGETHER)
            for h in range(0, heads, TOGETHER):
                s = later
                if h + TOGETHER < heads:
                    later = scores(h + TOGETHER, TOGETHER)
                weights = jnp.exp2(s * SCALE).astype(jnp.bfloat16)
                at = stack(h, TOGETHER)
                state_out[0, 0, :, at] = state_ref[0, 0, :, at] + times(values, weights)

        @pl.when(jnp.logical_not(near))
        def _():
            reach_out[...] = jnp.full(reach_out.shape, FAR, jnp.float32)
            live_rows = lax.broadcasted_iota(jnp.int32, (count, rows), 0) < length
            for h in range(heads):
                s = jnp.where(live_rows, scores(h, 1), NEVER)
                old = state_ref[0, 0, :, stack(h, 1)]
                old_peak = old[SHIFT_ROW : SHIFT_ROW + 1]
                peak = jnp.maximum(old_peak, jnp.max(s, axis=0, keepdims=True))
                weights = jnp.exp2((s - peak) * SCALE).astype(jnp.bfloat16)
                new = old * jnp.exp2((old_peak - peak) * SCALE) + times(values, weights)
                state_out[0, 0, :, stack(h, 1)] = keep_shift(new, peak)

    @pl.when(jnp.logical_not(wanted))
    def _():
        reach_out[...] = reach_ref[...]
        state_out[...] = state_ref[...]

    @pl.when(completes | jnp.logical_not(wanted))
    def _():
        for h in range(heads):
            share = state_out[0, 0, :HD, stack(h, 1)] * (1.0 / state_out[0, 0, HD : HD + 1, stack(h, 1)])
            out_ref[0, :, head_columns(h)] = share.astype(out_ref.dtype).T


def response_attention(shift, plan, query, kv, state, out):
    pairs, rows, width = query.shape
    steps = kv.shape[1] // HD
    step_width = width // steps
    stacked = step_width // HD * rows
    count = kv.shape[0] // 2
    pair_at = shift * FIELDS + 1
    state_specs = [
        pl.BlockSpec((1, 1, size, columns), lambda g, plan: (plan[pair_at], g, 0, 0))
        for size, columns in ((HD, stacked), (8, HD), (HD + EXTRA_ROWS, stacked))
    ]
    operands = [plan, kv, *state]
    in_specs = [pl.BlockSpec((2 * count, HD), lambda g, plan: (0, g)), *state_specs]
    aliases = {3: 0, 4: 1}
    if out is not None:
        aliases[len(operands)] = 2
        operands.append(out)
        in_specs.append(ANY)
    results = pl.pallas_call(
        functools.partial(response_kernel, shift),
        grid_spec=pltpu.PrefetchScalarGridSpec(
            num_scalar_prefetch=1,
            grid=(steps,),
            in_specs=in_specs,
            out_specs=state_specs[1:]
            + [pl.BlockSpec((1, rows, step_width), lambda g, plan: (plan[pair_at], 0, g))],
        ),
        out_shape=state_shapes(pairs, steps, stacked)[1:]
        + [jax.ShapeDtypeStruct(query.shape, jnp.bfloat16)],
        input_output_aliases=aliases,
        compiler_params=params("arbitrary"),
        cost_estimate=hint(
            6 * width * rows * count, rows * width * 12, width // HD * rows * count
        ),
        name="response_attention",
    )(*operands)
    return [state[0], *results[:2]], results[2]


def local(
    rubric_query,
    rubric_key,
    rubric_value,
    response_states,
    key_weight,
    value_weight,
    owner_slot,
    response_length,
    pair_table,
):
    groups = lax.axis_size("dp")
    stored, length, depth = response_states.shape
    pairs = rubric_query.shape[0]
    tensor = lax.axis_size("tensor")
    width = key_weight.shape[1] // tensor
    me = lax.axis_index("dp").astype(jnp.int32)
    own_half = lax.axis_index("tensor").astype(jnp.int32)
    other_half = 1 - own_half
    rows = response_states.reshape(stored * length, depth)
    swap = [(0, 1), (1, 0)]
    order = arrival_order(groups)
    place = jnp.array([0] + [1 + order.index(s) for s in range(1, groups)], jnp.int32)
    tables = [owner_slot, response_length, pair_table.T, place]

    plan = make_plan(me, tables, groups, stored)
    def other_columns(part):
        return lax.dynamic_slice_in_dim(part, other_half * width, width, 1)

    own_keys = times(rows, key_weight)
    keys_in = lax.ppermute(other_columns(own_keys), "tensor", swap)
    own_values = times(rows, value_weight)
    values_in = lax.ppermute(other_columns(own_values), "tensor", swap)
    blocks = finish(
        plan, own_half, own_keys, own_values, keys_in, values_in, groups, length
    )
    arrived = {0: blocks[0]}

    def send(shifts, *after):
        for shift in shifts:
            block = lax.optimization_barrier((blocks[shift], *after))[0]
            arrived[shift] = lax.ppermute(block, "dp", [(g, g ^ shift) for g in range(groups)])

    send(order[:2])
    half = pairs // 2
    state = rubric_attention(
        0, half, rubric_query, rubric_key, rubric_value, (), blocks[0]
    )
    send(order[2:4], state[1])
    state = rubric_attention(
        half, pairs - half, rubric_query, rubric_key, rubric_value, state, arrived[order[1]]
    )
    state, out = response_attention(0, plan, rubric_query, blocks[0], state, None)
    for at in range(0, len(order), 2):
        send(order[at + 4 : at + 6], arrived[order[at]], state[1])
        for shift in order[at : at + 2]:
            state, out = response_attention(
                shift, plan, rubric_query, arrived[shift], state, out
            )
    return out


def solution(mesh):
    return jax.shard_map(
        local,
        mesh=mesh,
        in_specs=(
            P(("rep", "dp"), None, "tensor"),
            P(("rep", "dp"), None, "tensor"),
            P(("rep", "dp"), None, "tensor"),
            P(("rep", "dp"), None, "tensor"),
            P("tensor", None),
            P("tensor", None),
            P("rep"),
            P("rep"),
            P("rep", None),
        ),
        out_specs=P(("rep", "dp"), None, "tensor"),
        check_vma=False,
    )
```

profile of v0, /device:TPU:0, one launch (start us, length us, event | category | flops | bytes accessed | tf_op | source)
XLA Modules:
  0.0 114.5 jit_solution(5858951691884633609)
XLA Ops:
  0.0 8.3 %fusion.1.own_values_ref = f32[1024,512]{1,0:T(8,128)S(1)} fusion(bf16[1024,4096]{1,0:T(8,128)(2,1)} %bitcast.9, bf16[4096,512]{1,0:T(8,128)(2,1)} %param.15), kind=kOutput, calls=%fused_computation.3 | convolution fusion | flops 4294967296 | bytes 14680064 | tf_op jit(solution)/shard_map/dot_general | solution.py:117
  8.3 1.1 constant_dynamic-slice_fusion
  9.8 4.5 %fusion.own_keys_ref = f32[1024,512]{1,0:T(8,128)S(1)} fusion(bf16[1024,4096]{1,0:T(8,128)(2,1)S(1)} %bitcast.10, bf16[4096,512]{1,0:T(8,128)(2,1)S(1)} %copy-done.7), kind=kOutput, calls=%fused_computation.2 | convolution fusion | flops 4294967296 | bytes 14680064 | tf_op jit(solution)/shard_map/dot_general | solution.py:117
  14.3 1.1 constant_dynamic-slice_fusion.1
  15.4 1.3 %copy-done = f32[1024,512]{1,0:T(8,128)} copy-done((f32[1024,512]{1,0:T(8,128)}, f32[1024,512]{1,0:T(8,128)S(1)}, u32[]{:S(2)}) %copy-start) | copy-done | bytes 2097176
  16.8 1.4 %plan.1.plan_ref = s32[40]{0:T(128)} custom-call(s32[1]{0:T(128)} %bitcast.me_ref, s32[32]{0:T(128)} %owner_ref.1, s32[32]{0:T(128)} %length_ref.1, s32[2,32]{1,0:T(2,128)} %bitcast.8, s32[8]{0:T(128)} %constant.18.clone.place_ref), custom_call_target="tpu_custom_call" | custom-call | tf_op jit(solution)/shard_map/plan/pallas_call | solution.py:79
  18.2 1.5 %collective-permute-done.keys_ref = f32[1024,256]{1,0:T(8,128)} collective-permute-done((f32[1024,256]{1,0:T(8,128)}, f32[1024,256]{1,0:T(8,128)}, u32[]{:S(2)}, u32[]{:S(2)}) %collective-permute-start) | collective-permute-done | bytes 1048608 | tf_op jit(solution)/shard_map/ppermute | solution.py:354
  19.7 1.6 %copy-done.1 = f32[1024,512]{1,0:T(8,128)S(1)} copy-done((f32[1024,512]{1,0:T(8,128)S(1)}, f32[1024,512]{1,0:T(8,128)}, u32[]{:S(2)}) %copy-start.1) | copy-done | bytes 2097176
  22.0 1.9 %finish.1 = (bf16[512,256]{1,0:T(8,128)(2,1)S(1)}, bf16[512,256]{1,0:T(8,128)(2,1)S(1)}, bf16[512,256]{1,0:T(8,128)(2,1)S(1)}, bf16[512,256]{1,0:T(8,128)(2,1)S(...) custom-call(s32[40]{0:T(128)S(1)} %copy-done.5, ...), custom_call_target="tpu_custom_call" | custom-call | flops 1048576 | bytes 6291456 | tf_op jit(solution)/shard_map/finish/pallas_call | solution.py:103
  23.9 3.8 %collective-permute-start.3 = (bf16[512,256]{1,0:T(8,128)(2,1)S(1)}, bf16[512,256]{1,0:T(8,128)(2,1)S(1)}, u32[]{:S(2)}, u32[]{:S(2)}) collective-permute-start(bf16[512,256]{1,0:T(8,128)(2,1)S(1)} %get-tuple-element.51), channel_id=1, source_target_pairs={{0,6},{2,4},{4,2},{6,0},{8,14},{10,12},{12,10},{14,8},{1,7},{3,5},... | collective-permute-start | bytes 786440 | tf_op jit(solution)/shard_map/ppermute | solution.py:365
  27.7 2.4 %collective-permute-start.4 = (bf16[512,256]{1,0:T(8,128)(2,1)S(1)}, bf16[512,256]{1,0:T(8,128)(2,1)S(1)}, u32[]{:S(2)}, u32[]{:S(2)}) collective-permute-start(bf16[512,256]{1,0:T(8,128)(2,1)S(1)} %get-tuple-element.55), channel_id=1, source_target_pairs={{0,14},{2,12},{4,10},{6,8},{8,6},{10,4},{12,2},{14,0},{1,15},{3,13... | collective-permute-start | bytes 786440 | tf_op jit(solution)/shard_map/ppermute | solution.py:365
  30.1 11.4 %rubric_attention.2 = (bf16[4,2,128,2048]{3,2,1,0:T(8,128)(2,1)S(1)}, f32[4,2,8,128]{3,2,1,0:T(8,128)S(1)}, f32[4,2,144,2048]{3,2,1,0:T(8,128)S(1)}) custom-call(bf16[4,256,2048]{2,1,0:T(8,128)(2,1)S(1)} %copy-done.2, bf16[4,256,256]{2,1,0:T(8,128)(2,1)S(1)} %copy-done.3, bf16[4,256,256]{2,1,0:T(8,128)(2,1)S(1)} %copy-done.4, ...), custom_call_target="tpu_custom_call" | custom-call | flops 1610612736 | bytes 8388608 | tf_op jit(solution)/shard_map/rubric_attention/pallas_call | solution.py:205
  41.5 1.4 %collective-permute-start.2 = (bf16[512,256]{1,0:T(8,128)(2,1)S(1)}, bf16[512,256]{1,0:T(8,128)(2,1)S(1)}, u32[]{:S(2)}, u32[]{:S(2)}) collective-permute-start(bf16[512,256]{1,0:T(8,128)(2,1)S(1)} %get-tuple-element.50), channel_id=1, source_target_pairs={{0,12},{2,14},{4,8},{6,10},{8,4},{10,6},{12,0},{14,2},{1,13},{3,15... | collective-permute-start | bytes 786440 | tf_op jit(solution)/shard_map/ppermute | solution.py:365
  42.9 11.4 %rubric_attention.3 = (bf16[4,2,128,2048]{3,2,1,0:T(8,128)(2,1)S(1)}, f32[4,2,8,128]{3,2,1,0:T(8,128)S(1)}, f32[4,2,144,2048]{3,2,1,0:T(8,128)S(1)}) custom-call(bf16[4,256,2048]{2,1,0:T(8,128)(2,1)S(1)} %copy-done.2, bf16[4,256,256]{2,1,0:T(8,128)(2,1)S(1)} %copy-done.3, ...), custom_call_target="tpu_custom_call", output_to_operand_aliasing={{0}: (4, {}), {1}: (5, {}), {2}: (6, {})} | custom-call | flops 1610612736 | bytes 8388608 | tf_op jit(solution)/shard_map/rubric_attention/pallas_call | solution.py:205
  54.4 6.9 %response_attention.8 = (f32[4,2,8,128]{3,2,1,0:T(8,128)S(1)}, f32[4,2,144,2048]{3,2,1,0:T(8,128)S(1)}, bf16[4,256,2048]{2,1,0:T(8,128)(2,1)}) custom-call(s32[40]{0:T(128)S(1)} %copy-done.5, bf16[512,256]{1,0:T(8,128)(2,1)S(1)} %get-tuple-element.48.refs_0_.kv_ref, ...), custom_call_target="tpu_custom_call", output_to_operand_aliasing={{0}: (3, {}), {1}: (4, {})} | custom-call | flops 805306368 | bytes 6291456 | tf_op jit(solution)/shard_map/response_attention/pallas_call | solution.py:303
  61.2 1.5 %collective-permute-start.6 = (bf16[512,256]{1,0:T(8,128)(2,1)S(1)}, bf16[512,256]{1,0:T(8,128)(2,1)S(1)}, u32[]{:S(2)}, u32[]{:S(2)}) collective-permute-start(bf16[512,256]{1,0:T(8,128)(2,1)S(1)} %get-tuple-element.67), channel_id=1, source_target_pairs={{0,2},{2,0},{4,6},{6,4},{8,10},{10,8},{12,14},{14,12},{1,3},{3,1},... | collective-permute-start | bytes 786440 | tf_op jit(solution)/shard_map/ppermute | solution.py:365
  62.8 3.0 %collective-permute-start.7 = (bf16[512,256]{1,0:T(8,128)(2,1)S(1)}, bf16[512,256]{1,0:T(8,128)(2,1)S(1)}, u32[]{:S(2)}, u32[]{:S(2)}) collective-permute-start(bf16[512,256]{1,0:T(8,128)(2,1)S(1)} %get-tuple-element.69), channel_id=1, source_target_pairs={{0,10},{2,8},{4,14},{6,12},{8,2},{10,0},{12,6},{14,4},{1,11},{3,9}... | collective-permute-start | bytes 786440 | tf_op jit(solution)/shard_map/ppermute | solution.py:365
  65.7 6.7 %response_attention.9 = (f32[4,2,8,128]{3,2,1,0:T(8,128)S(1)}, f32[4,2,144,2048]{3,2,1,0:T(8,128)S(1)}, bf16[4,256,2048]{2,1,0:T(8,128)(2,1)}) custom-call(s32[40]{0:T(128)S(1)} %copy-done.5, bf16[512,256]{1,0:T(8,128)(2,1)S(1)} %collective-permute-done.4.kv_ref, ...), custom_call_target="tpu_custom_call", output_to_operand_aliasing={{0}: (3, {}), {1}: (4, {}), {2}: (5, {})} | custom-call | flops 805306368 | bytes 6291456 | tf_op jit(solution)/shard_map/response_attention/pallas_call | solution.py:303
  72.4 6.7 %response_attention.10 = (f32[4,2,8,128]{3,2,1,0:T(8,128)S(1)}, f32[4,2,144,2048]{3,2,1,0:T(8,128)S(1)}, bf16[4,256,2048]{2,1,0:T(8,128)(2,1)}) custom-call(s32[40]{0:T(128)S(1)} %copy-done.5, bf16[512,256]{1,0:T(8,128)(2,1)S(1)} %collective-permute-done.3.refs_0_.kv_ref, ...), custom_call_target="tpu_custom_call", output_to_operand_aliasing={{0}: (3, {}), {1}: (4, {}), {2}: (5, {})} | custom-call | flops 805306368 | bytes 6291456 | tf_op jit(solution)/shard_map/response_attention/pallas_call | solution.py:303
  79.2 6.7 %response_attention.11 = (f32[4,2,8,128]{3,2,1,0:T(8,128)S(1)}, f32[4,2,144,2048]{3,2,1,0:T(8,128)S(1)}, bf16[4,256,2048]{2,1,0:T(8,128)(2,1)}) custom-call(s32[40]{0:T(128)S(1)} %copy-done.5, bf16[512,256]{1,0:T(8,128)(2,1)S(1)} %collective-permute-done.2.kv_ref, ...), custom_call_target="tpu_custom_call", output_to_operand_aliasing={{0}: (3, {}), {1}: (4, {}), {2}: (5, {})} | custom-call | flops 805306368 | bytes 6291456 | tf_op jit(solution)/shard_map/response_attention/pallas_call | solution.py:303
  85.9 7.3 %response_attention.12 = (f32[4,2,8,128]{3,2,1,0:T(8,128)S(1)}, f32[4,2,144,2048]{3,2,1,0:T(8,128)S(1)}, bf16[4,256,2048]{2,1,0:T(8,128)(2,1)}) custom-call(s32[40]{0:T(128)S(1)} %copy-done.5, bf16[512,256]{1,0:T(8,128)(2,1)S(1)} %collective-permute-done.8.kv_ref, ...), custom_call_target="tpu_custom_call", output_to_operand_aliasing={{0}: (3, {}), {1}: (4, {}), {2}: (5, {})} | custom-call | flops 805306368 | bytes 6291456 | tf_op jit(solution)/shard_map/response_attention/pallas_call | solution.py:303
  93.2 7.1 %response_attention.13 = (f32[4,2,8,128]{3,2,1,0:T(8,128)S(1)}, f32[4,2,144,2048]{3,2,1,0:T(8,128)S(1)}, bf16[4,256,2048]{2,1,0:T(8,128)(2,1)}) custom-call(s32[40]{0:T(128)S(1)} %copy-done.5, bf16[512,256]{1,0:T(8,128)(2,1)S(1)} %collective-permute-done.7.kv_ref, ...), custom_call_target="tpu_custom_call", output_to_operand_aliasing={{0}: (3, {}), {1}: (4, {}), {2}: (5, {})} | custom-call | flops 805306368 | bytes 6291456 | tf_op jit(solution)/shard_map/response_attention/pallas_call | solution.py:303
  100.3 7.1 %response_attention.14 = (f32[4,2,8,128]{3,2,1,0:T(8,128)S(1)}, f32[4,2,144,2048]{3,2,1,0:T(8,128)S(1)}, bf16[4,256,2048]{2,1,0:T(8,128)(2,1)}) custom-call(s32[40]{0:T(128)S(1)} %copy-done.5, bf16[512,256]{1,0:T(8,128)(2,1)S(1)} %collective-permute-done.6.kv_ref, ...), custom_call_target="tpu_custom_call", output_to_operand_aliasing={{0}: (3, {}), {1}: (4, {}), {2}: (5, {})} | custom-call | flops 805306368 | bytes 6291456 | tf_op jit(solution)/shard_map/response_attention/pallas_call | solution.py:303
  107.4 7.1 %response_attention.15 = (f32[4,2,8,128]{3,2,1,0:T(8,128)S(1)}, f32[4,2,144,2048]{3,2,1,0:T(8,128)S(1)}, bf16[4,256,2048]{2,1,0:T(8,128)(2,1)}) custom-call(s32[40]{0:T(128)S(1)} %copy-done.5, bf16[512,256]{1,0:T(8,128)(2,1)S(1)} %collective-permute-done.5.kv_ref, ...), custom_call_target="tpu_custom_call", output_to_operand_aliasing={{0}: (3, {}), {1}: (4, {}), {2}: (5, {})} | custom-call | flops 805306368 | bytes 6291456 | tf_op jit(solution)/shard_map/response_attention/pallas_call | solution.py:303
  (26 shorter events, 1.3 us)
Async XLA Ops:
  0.0 9.8 %copy-start.6 = (bf16[4,256,4096]{2,1,0:T(8,128)(2,1)S(1)}, bf16[4,256,4096]{2,1,0:T(8,128)(2,1)}, u32[]{:S(2)}) copy-start(bf16[4,256,4096]{2,1,0:T(8,128)(2,1)} %param.13) | copy-start | bytes 25165828
  0.0 9.8 %copy-start.7 = (bf16[4096,512]{1,0:T(8,128)(2,1)S(1)}, bf16[4096,512]{1,0:T(8,128)(2,1)}, u32[]{:S(2)}) copy-start(bf16[4096,512]{1,0:T(8,128)(2,1)} %param.14) | copy-start | bytes 12582916
  9.4 8.8 %collective-permute-start.1 = (f32[1024,256]{1,0:T(8,128)}, f32[1024,256]{1,0:T(8,128)S(1)}, u32[]{:S(2)}, u32[]{:S(2)}) collective-permute-start(f32[1024,256]{1,0:T(8,128)} %constant_dynamic-slice_fusion), channel_id=1, source_target_pairs={{0,1},{1,0},{2,3},{3,2},{4,5},{5,4},{6,7},{7,6},{8,9},{9,8},{10,11... | collective-permute-start | bytes 3145736 | tf_op jit(solution)/shard_map/ppermute | solution.py:356
  15.4 1.3 %copy-start = (f32[1024,512]{1,0:T(8,128)}, f32[1024,512]{1,0:T(8,128)S(1)}, u32[]{:S(2)}) copy-start(f32[1024,512]{1,0:T(8,128)S(1)} %fusion.own_keys_ref) | copy-start | bytes 6291460
  16.7 3.0 %collective-permute-start = (f32[1024,256]{1,0:T(8,128)}, f32[1024,256]{1,0:T(8,128)}, u32[]{:S(2)}, u32[]{:S(2)}) collective-permute-start(f32[1024,256]{1,0:T(8,128)} %constant_dynamic-slice_fusion.1), channel_id=1, source_target_pairs={{0,1},{1,0},{2,3},{3,2},{4,5},{5,4},{6,7},{7,6},{8,9},{9,8},{10,11... | collective-permute-start | bytes 3145736 | tf_op jit(solution)/shard_map/ppermute | solution.py:354
  19.7 1.6 %copy-start.1 = (f32[1024,512]{1,0:T(8,128)S(1)}, f32[1024,512]{1,0:T(8,128)}, u32[]{:S(2)}) copy-start(f32[1024,512]{1,0:T(8,128)} %copy-done) | copy-start | bytes 6291460
  21.3 0.7 copy-start.5
  22.0 8.1 %copy-start.2 = (bf16[4,256,2048]{2,1,0:T(8,128)(2,1)S(1)}, bf16[4,256,2048]{2,1,0:T(8,128)(2,1)}, u32[]{:S(2)}) copy-start(bf16[4,256,2048]{2,1,0:T(8,128)(2,1)} %q_ref.3) | copy-start | bytes 12582916
  22.0 8.1 %copy-start.3 = (bf16[4,256,256]{2,1,0:T(8,128)(2,1)S(1)}, bf16[4,256,256]{2,1,0:T(8,128)(2,1)}, u32[]{:S(2)}) copy-start(bf16[4,256,256]{2,1,0:T(8,128)(2,1)} %k_ref.3) | copy-start | bytes 1572868
  22.0 8.1 %copy-start.4 = (bf16[4,256,256]{2,1,0:T(8,128)(2,1)S(1)}, bf16[4,256,256]{2,1,0:T(8,128)(2,1)}, u32[]{:S(2)}) copy-start(bf16[4,256,256]{2,1,0:T(8,128)(2,1)} %v_ref.3) | copy-start | bytes 1572868
  23.9 19.0 %collective-permute-start.3 = (bf16[512,256]{1,0:T(8,128)(2,1)S(1)}, bf16[512,256]{1,0:T(8,128)(2,1)S(1)}, u32[]{:S(2)}, u32[]{:S(2)}) collective-permute-start(bf16[512,256]{1,0:T(8,128)(2,1)S(1)} %get-tuple-element.51), channel_id=1, source_target_pairs={{0,6},{2,4},{4,2},{6,0},{8,14},{10,12},{12,10},{14,8},{1,7},{3,5},... | collective-permute-start | bytes 786440 | tf_op jit(solution)/shard_map/ppermute | solution.py:365
  27.7 33.6 %collective-permute-start.4 = (bf16[512,256]{1,0:T(8,128)(2,1)S(1)}, bf16[512,256]{1,0:T(8,128)(2,1)S(1)}, u32[]{:S(2)}, u32[]{:S(2)}) collective-permute-start(bf16[512,256]{1,0:T(8,128)(2,1)S(1)} %get-tuple-element.55), channel_id=1, source_target_pairs={{0,14},{2,12},{4,10},{6,8},{8,6},{10,4},{12,2},{14,0},{1,15},{3,13... | collective-permute-start | bytes 786440 | tf_op jit(solution)/shard_map/ppermute | solution.py:365
  41.5 37.6 %collective-permute-start.2 = (bf16[512,256]{1,0:T(8,128)(2,1)S(1)}, bf16[512,256]{1,0:T(8,128)(2,1)S(1)}, u32[]{:S(2)}, u32[]{:S(2)}) collective-permute-start(bf16[512,256]{1,0:T(8,128)(2,1)S(1)} %get-tuple-element.50), channel_id=1, source_target_pairs={{0,12},{2,14},{4,8},{6,10},{8,4},{10,6},{12,0},{14,2},{1,13},{3,15... | collective-permute-start | bytes 786440 | tf_op jit(solution)/shard_map/ppermute | solution.py:365
  42.9 42.9 %collective-permute-start.8 = (bf16[512,256]{1,0:T(8,128)(2,1)S(1)}, bf16[512,256]{1,0:T(8,128)(2,1)S(1)}, u32[]{:S(2)}, u32[]{:S(2)}) collective-permute-start(bf16[512,256]{1,0:T(8,128)(2,1)S(1)} %get-tuple-element.71), channel_id=1, source_target_pairs={{0,4},{2,6},{4,0},{6,2},{8,12},{10,14},{12,8},{14,10},{1,5},{3,7},... | collective-permute-start | bytes 786440 | tf_op jit(solution)/shard_map/ppermute | solution.py:365
  61.2 39.0 %collective-permute-start.6 = (bf16[512,256]{1,0:T(8,128)(2,1)S(1)}, bf16[512,256]{1,0:T(8,128)(2,1)S(1)}, u32[]{:S(2)}, u32[]{:S(2)}) collective-permute-start(bf16[512,256]{1,0:T(8,128)(2,1)S(1)} %get-tuple-element.67), channel_id=1, source_target_pairs={{0,2},{2,0},{4,6},{6,4},{8,10},{10,8},{12,14},{14,12},{1,3},{3,1},... | collective-permute-start | bytes 786440 | tf_op jit(solution)/shard_map/ppermute | solution.py:365
  62.8 30.4 %collective-permute-start.7 = (bf16[512,256]{1,0:T(8,128)(2,1)S(1)}, bf16[512,256]{1,0:T(8,128)(2,1)S(1)}, u32[]{:S(2)}, u32[]{:S(2)}) collective-permute-start(bf16[512,256]{1,0:T(8,128)(2,1)S(1)} %get-tuple-element.69), channel_id=1, source_target_pairs={{0,10},{2,8},{4,14},{6,12},{8,2},{10,0},{12,6},{14,4},{1,11},{3,9}... | collective-permute-start | bytes 786440 | tf_op jit(solution)/shard_map/ppermute | solution.py:365
  79.1 28.3 %collective-permute-start.5 = (bf16[512,256]{1,0:T(8,128)(2,1)S(1)}, bf16[512,256]{1,0:T(8,128)(2,1)S(1)}, u32[]{:S(2)}, u32[]{:S(2)}) collective-permute-start(bf16[512,256]{1,0:T(8,128)(2,1)S(1)} %get-tuple-element.65), channel_id=1, source_target_pairs={{0,8},{2,10},{4,12},{6,14},{8,0},{10,2},{12,4},{14,6},{1,9},{3,11}... | collective-permute-start | bytes 786440 | tf_op jit(solution)/shard_map/ppermute | solution.py:365
where the time goes:
time: 115 us; the launch traced here: 114 us
  Pallas kernels  81.7 us (71%)
  matrix products  12.7 us (11%)
  starting transfers between devices  12.7 us (11%)
  local copies, waits for them, and re-layouts  5.76 us (5%)
  waiting for transfers between devices  1.51 us (1%)
    pallas_call x8, Pallas kernels, response_attention(): pl.pallas_call(functools.partial(response_kernel, shift), grid_spec=pltpu...  55.5 us
    pallas_call x2, Pallas kernels, rubric_attention(): pl.pallas_call(rubric_kernel, grid=(some, steps), in_specs=[across(step_w...  22.8 us
    dot_general x2, matrix products, times(): return jnp.dot(a, b, preferred_element_type=jnp.float32)  12.7 us
    ppermute x7, starting transfers between devices, send(): lax.ppermute(block, 'dp', [(g, g ^ shift) for g in range(groups)])  12.2 us
    unnamed x16, local copies, waits for them, and re-layouts  3.59 us
  transfers between devices with their start and end apart: 9, of which 1 were waited for; matrix products, arithmetic and copies ran while one was open for 5% of the time, Pallas kernels for 63%

commit v1 on v0

--- a/solution.py
+++ b/solution.py
@@ -13,6 +13,8 @@
 MIB = 1024 * 1024
 FIELDS = 5
 NEVER = -1e30
+SUB_ROWS = 128
+PART = 1
 NEAR = 100.0
 FAR = 1e30
 TOGETHER = 2
@@ -29,19 +31,21 @@
     )
 
 
-def hint(flops, bytes_accessed, transcendentals):
+def hint(flops, bytes_accessed, transcendentals, part=1):
     return pl.CostEstimate(
-        flops=flops, bytes_accessed=bytes_accessed, transcendentals=transcendentals
-    )
-
-
-def arrival_order(groups):
-    far = list(range(groups - 1, groups // 2 - 1, -1))
-    near = list(range(groups // 2 - 1, 0, -1))
-    order = []
-    for at in range(len(far)):
-        order += far[at : at + 1] + near[at : at + 1]
-    return order
+        flops=flops // part,
+        bytes_accessed=bytes_accessed // part,
+        transcendentals=transcendentals // part,
+    )
+
+
+def partners(groups):
+    return list(range(groups - 1, groups // 2 - 1, -1)), list(range(groups // 2 - 1, 0, -1))
+
+
+def order_of_use(groups):
+    far, near = partners(groups)
+    return [0] + near[:2] + far[:-1] + near[2:] + far[-1:]
 
 
 def write_plan(groups, stored, me, owner_ref, length_ref, table_ref, place_ref, plan_ref):
@@ -71,46 +75,64 @@
         plan_ref[shift * FIELDS + 4] = later.astype(jnp.int32)
 
 
-def plan_kernel(groups, stored, me_ref, owner_ref, length_ref, table_ref, place_ref, plan_ref):
+def project_rows_kernel(groups, stored, half_ref, me_ref, owner_ref, length_ref, table_ref, place_ref, x_ref, key_ref, value_ref, out_ref, plan_ref):
     write_plan(groups, stored, me_ref[0], owner_ref, length_ref, table_ref, place_ref, plan_ref)
-
-
-def make_plan(me, tables, groups, stored):
+    width = key_ref.shape[1]
+    for at in range(0, x_ref.shape[0], SUB_ROWS):
+        part = slice(at, at + SUB_ROWS)
+        out_ref[part, :width] = times(x_ref[part, :], key_ref[...])
+        out_ref[part, width:] = times(x_ref[part, :], value_ref[...])
+
+
+def project_and_plan(rows, key_weight, value_weight, half, width, me, tables, groups, stored):
+    total, depth = rows.shape
+    block = 256
+    weight_spec = pl.BlockSpec((depth, width), lambda i, half, me: (0, half[0]))
     return pl.pallas_call(
-        functools.partial(plan_kernel, groups, stored),
-        out_shape=jax.ShapeDtypeStruct((groups * FIELDS,), jnp.int32),
-        in_specs=[SMEM] * 5,
-        out_specs=SMEM,
-        name="plan",
-    )(me[None], *tables)
-
-
-def finish_kernel(length, plan_ref, half_ref, own_keys_ref, own_values_ref, keys_ref, values_ref, *out_refs):
-    width = keys_ref.shape[1]
-    own_columns = pl.ds(pl.multiple_of(half_ref[0] * width, width), width)
+        functools.partial(project_rows_kernel, groups, stored),
+        grid_spec=pltpu.PrefetchScalarGridSpec(
+            num_scalar_prefetch=2,
+            grid=(total // block,),
+            in_specs=[SMEM] * len(tables)
+            + [pl.BlockSpec((block, depth), lambda i, half, me: (i, 0)), weight_spec, weight_spec],
+            out_specs=[pl.BlockSpec((block, 2 * width), lambda i, half, me: (i, 0)), SMEM],
+        ),
+        out_shape=[
+            jax.ShapeDtypeStruct((total, 2 * width), jnp.float32),
+            jax.ShapeDtypeStruct((groups * FIELDS,), jnp.int32),
+        ],
+        compiler_params=params("arbitrary", vmem=60),
+        cost_estimate=hint(
+            4 * total * depth * width, 2 * total * depth + 4 * depth * width + 8 * total * width, 0
+        ),
+        name="other_half",
+    )(half[None], me[None], *tables, rows, key_weight, value_weight)
+
+
+def finish_kernel(length, width, plan_ref, own_keys_ref, own_values_ref, other_ref, *out_refs):
     for shift, out_ref in enumerate(out_refs):
         start = pl.multiple_of(plan_ref[shift * FIELDS] * length, length)
         rows = pl.ds(start, length)
-        for at, (own_ref, other_ref) in enumerate(
-            ((own_keys_ref, keys_ref), (own_values_ref, values_ref))
-        ):
-            total = own_ref[rows, own_columns] + other_ref[rows, :]
+        for at, own_ref in enumerate((own_keys_ref, own_values_ref)):
+            total = own_ref[rows, :] + other_ref[rows, at * width : (at + 1) * width]
             out_ref[at * length : (at + 1) * length, :] = total.astype(out_ref.dtype)
 
 
-def finish(plan, half, own_keys, own_values, other_keys, other_values, groups, length):
-    total, width = other_keys.shape
+def finish(plan, own_keys, own_values, other, groups, length, name):
+    total, width = own_keys.shape
     return pl.pallas_call(
-        functools.partial(finish_kernel, length),
+        functools.partial(finish_kernel, length, width),
         out_shape=[jax.ShapeDtypeStruct((2 * length, width), jnp.bfloat16)] * groups,
-        in_specs=[SMEM] * 2 + [WHOLE] * 4,
+        in_specs=[SMEM, WHOLE, WHOLE, WHOLE],
         out_specs=[WHOLE] * groups,
         compiler_params=params(),
         cost_estimate=hint(
-            2 * groups * length * width, 16 * total * width + 4 * groups * length * width, 0
-        ),
-        name="finish",
-    )(plan, half[None], own_keys, own_values, other_keys, other_values)
+            2 * groups * length * width,
+            16 * total * width + 4 * groups * length * width,
+            0,
+        ),
+        name=name,
+    )(plan, own_keys, own_values, other)
 
 
 def times(a, b):
@@ -217,6 +239,7 @@
             6 * some * width * rows * count,
             some * rows * width * 8,
             some * width // HD * rows * count,
+            part=PART,
         ),
         name="rubric_attention",
     )(query, key, value, after, *state)
@@ -314,7 +337,8 @@
         input_output_aliases=aliases,
         compiler_params=params("arbitrary"),
         cost_estimate=hint(
-            6 * width * rows * count, rows * width * 12, width // HD * rows * count
+            6 * width * rows * count, rows * width * 12, width // HD * rows * count,
+            part=PART,
         ),
         name="response_attention",
     )(*operands)
@@ -342,21 +366,20 @@
     other_half = 1 - own_half
     rows = response_states.reshape(stored * length, depth)
     swap = [(0, 1), (1, 0)]
-    order = arrival_order(groups)
-    place = jnp.array([0] + [1 + order.index(s) for s in range(1, groups)], jnp.int32)
+    far, near = partners(groups)
+    order = order_of_use(groups)
+    place = jnp.array([order.index(shift) for shift in range(groups)], jnp.int32)
     tables = [owner_slot, response_length, pair_table.T, place]
 
-    plan = make_plan(me, tables, groups, stored)
-    def other_columns(part):
-        return lax.dynamic_slice_in_dim(part, other_half * width, width, 1)
-
-    own_keys = times(rows, key_weight)
-    keys_in = lax.ppermute(other_columns(own_keys), "tensor", swap)
-    own_values = times(rows, value_weight)
-    values_in = lax.ppermute(other_columns(own_values), "tensor", swap)
-    blocks = finish(
-        plan, own_half, own_keys, own_values, keys_in, values_in, groups, length
-    )
+    other, plan = project_and_plan(
+        rows, key_weight, value_weight, other_half, width, me, tables, groups, stored
+    )
+    received = lax.ppermute(other, "tensor", swap)
+    own_keys, own_values = (
+        times(rows, lax.dynamic_slice_in_dim(weight, own_half * width, width, 1))
+        for weight in (key_weight, value_weight)
+    )
+    blocks = finish(plan, own_keys, own_values, received, groups, length, "finish")
     arrived = {0: blocks[0]}
 
     def send(shifts, *after):
@@ -364,22 +387,27 @@
             block = lax.optimization_barrier((blocks[shift], *after))[0]
             arrived[shift] = lax.ppermute(block, "dp", [(g, g ^ shift) for g in range(groups)])
 
-    send(order[:2])
+    send(far[:1] + near[:1])
     half = pairs // 2
+    state = rubric_attention(0, half, rubric_query, rubric_key, rubric_value, (), blocks[0])
+    send(far[1:2] + near[1:2], state[1])
     state = rubric_attention(
-        0, half, rubric_query, rubric_key, rubric_value, (), blocks[0]
-    )
-    send(order[2:4], state[1])
-    state = rubric_attention(
-        half, pairs - half, rubric_query, rubric_key, rubric_value, state, arrived[order[1]]
-    )
-    state, out = response_attention(0, plan, rubric_query, blocks[0], state, None)
-    for at in range(0, len(order), 2):
-        send(order[at + 4 : at + 6], arrived[order[at]], state[1])
-        for shift in order[at : at + 2]:
-            state, out = response_attention(
-                shift, plan, rubric_query, arrived[shift], state, out
-            )
+        half, pairs - half, rubric_query, rubric_key, rubric_value, state, blocks[0]
+    )
+    send(far[2:3], state[1], arrived[near[0]])
+    to_send = [(shift, far[at]) for at, shift in enumerate(far[3:])]
+    to_send += [(shift, far[at + 1]) for at, shift in enumerate(near[2:])]
+    out = None
+    for shift in order:
+        while shift not in arrived:
+            last, before = to_send.pop(0)
+            send([last], state[1], arrived[before])
+        state, out = response_attention(
+            shift, plan, rubric_query, arrived[shift], state, out
+        )
+        for last, before in [entry for entry in to_send if entry[1] == shift]:
+            to_send.remove((last, before))
+            send([last], state[1], arrived[before])
     return out
 
 

time: 115 us -> 112 us (0.974)
  Pallas kernels: 81.7 us -> 88.6 us
  local copies, waits for them, and re-layouts: 5.76 us -> 1.1 us
  matrix products: 12.7 us -> 8.79 us
  waiting for transfers between devices: 1.51 us -> 0.02 us
    pallas_call x2, Pallas kernels: 3.36 us -> 10.4 us  [the longest x1 9.45 us: project_and_plan(): pl.pallas_call(functools.partial(project_rows_kernel, groups, stored), gr...]
    dot_general x2, matrix products: 12.7 us -> 8.79 us  [times(): return jnp.dot(a, b, preferred_element_type=jnp.float32)]
    unnamed x16 -> x12, local copies, waits for them, and re-layouts: 3.59 us -> 1.1 us
    dynamic_slice x2 -> x0, local copies, waits for them, and re-layouts: 2.16 us -> none  [other_columns(): return lax.dynamic_slice_in_dim(part, other_half * width, width, 1)]
    ppermute x2 -> x1, waiting for transfers between devices: 1.5 us -> 0.01 us  [local(): received = lax.ppermute(other, 'tensor', swap)]
  transfers between devices with their start and end apart: 9 -> 8, of which waited for: 1 -> 0; matrix products, arithmetic and copies ran while one was open for 5% -> 8% of each run, Pallas kernels for 63% -> 64%
where the time goes in v1:
time: 112 us
  Pallas kernels  88.6 us (79%)
  starting transfers between devices  13.1 us (12%)
  matrix products  8.79 us (8%)
    pallas_call x8, Pallas kernels, response_attention(): pl.pallas_call(functools.partial(response_kernel, shift), grid_spec=pltpu...  55.4 us
    pallas_call x2, Pallas kernels, rubric_attention(): pl.pallas_call(rubric_kernel, grid=(some, steps), in_specs=[across(step_w...  22.8 us
    ppermute x7, starting transfers between devices, send(): lax.ppermute(block, 'dp', [(g, g ^ shift) for g in range(groups)])  12.6 us
    pallas_call x1, Pallas kernels, project_and_plan(): pl.pallas_call(functools.partial(project_rows_kernel, groups, stored), gr...  9.45 us
    dot_general x2, matrix products, times(): return jnp.dot(a, b, preferred_element_type=jnp.float32)  8.79 us
  transfers between devices with their start and end apart: 8, of which 0 were waited for; matrix products, arithmetic and copies ran while one was open for 8% of the time, Pallas kernels for 64%

profile of v1, /device:TPU:0, one launch (start us, length us, event | category | flops | bytes accessed | tf_op | source)
XLA Modules:
  0.0 111.7 jit_solution(252559268766357869)
XLA Ops:
  0.0 9.4 %other_half.1 = (f32[1024,512]{1,0:T(8,128)}, s32[40]{0:T(128)}) custom-call(s32[1]{0:T(128)} %bitcast.half_ref, s32[1]{0:T(128)} %bitcast.1.me_ref, s32[32]{0:T(128)} %owner_ref.1, s32[32]{0:T(128)} %length_ref.1, s32[2,32]{1,0:T(2,128)} %bitcast.13, s32[8]{0:T(128)} %constant.18.clone.place_ref, bf16[1024,4096]{1,0:T(8,128)(2,1)} %bitcast.10, ...), custom_call_target="tpu_custom_call" | custom-call | flops 4294967296 | bytes 14680064 | tf_op jit(solution)/shard_map/other_half/pallas_call | solution.py:91
  9.4 0.5 collective-permute-start
  9.9 6.5 %fusion.4.own_keys_ref = f32[1024,256]{1,0:T(8,128)S(1)} fusion(bf16[1024,4096]{1,0:T(8,128)(2,1)} %bitcast.11, bf16[4096,512]{1,0:T(8,128)(2,1)} %key_ref.1, s32[]{:T(128)S(6)} %select_n.4), kind=kOutput, calls=%fused_computation.4 | convolution fusion | flops 2147483648 | bytes 11534340 | tf_op jit(solution)/shard_map/dot_general | solution.py:139
  16.4 1.1 copy-done.5
  17.5 2.3 %fusion.7.own_values_ref = f32[1024,256]{1,0:T(8,128)S(1)} fusion(bf16[1024,4096]{1,0:T(8,128)(2,1)S(1)} %bitcast.12, bf16[4096,512]{1,0:T(8,128)(2,1)S(1)} %copy-done.5, s32[]{:T(128)S(6)} %select_n.4), kind=kOutput, calls=%fused_computation.5 | convolution fusion | flops 2147483648 | bytes 11534340 | tf_op jit(solution)/shard_map/dot_general | solution.py:139
  19.8 0.0 copy-start
  19.8 0.0 collective-permute-done.other_ref
  19.9 0.9 finish.1
  20.8 5.6 %collective-permute-start.1 = (bf16[512,256]{1,0:T(8,128)(2,1)S(1)}, bf16[512,256]{1,0:T(8,128)(2,1)S(1)}, u32[]{:S(2)}, u32[]{:S(2)}) collective-permute-start(bf16[512,256]{1,0:T(8,128)(2,1)S(1)} %get-tuple-element.51), channel_id=1, source_target_pairs={{0,14},{2,12},{4,10},{6,8},{8,6},{10,4},{12,2},{14,0},{1,15},{3,13... | collective-permute-start | bytes 786440 | tf_op jit(solution)/shard_map/ppermute | solution.py:388
  26.4 11.4 %rubric_attention.2 = (bf16[4,2,128,2048]{3,2,1,0:T(8,128)(2,1)S(1)}, f32[4,2,8,128]{3,2,1,0:T(8,128)S(1)}, f32[4,2,144,2048]{3,2,1,0:T(8,128)S(1)}) custom-call(bf16[4,256,2048]{2,1,0:T(8,128)(2,1)S(1)} %copy-done, bf16[4,256,256]{2,1,0:T(8,128)(2,1)S(1)} %copy-done.1, bf16[4,256,256]{2,1,0:T(8,128)(2,1)S(1)} %copy-done.2, ...), custom_call_target="tpu_custom_call" | custom-call | flops 1610612736 | bytes 8388608 | tf_op jit(solution)/shard_map/rubric_attention/pallas_call | solution.py:227
  37.8 2.0 %collective-permute-start.2 = (bf16[512,256]{1,0:T(8,128)(2,1)S(1)}, bf16[512,256]{1,0:T(8,128)(2,1)S(1)}, u32[]{:S(2)}, u32[]{:S(2)}) collective-permute-start(bf16[512,256]{1,0:T(8,128)(2,1)S(1)} %get-tuple-element.58), channel_id=1, source_target_pairs={{0,4},{2,6},{4,0},{6,2},{8,12},{10,14},{12,8},{14,10},{1,5},{3,7},... | collective-permute-start | bytes 786440 | tf_op jit(solution)/shard_map/ppermute | solution.py:388
  39.9 0.1 collective-permute-start.5
  40.0 11.4 %rubric_attention.3 = (bf16[4,2,128,2048]{3,2,1,0:T(8,128)(2,1)S(1)}, f32[4,2,8,128]{3,2,1,0:T(8,128)S(1)}, f32[4,2,144,2048]{3,2,1,0:T(8,128)S(1)}) custom-call(bf16[4,256,2048]{2,1,0:T(8,128)(2,1)S(1)} %copy-done, bf16[4,256,256]{2,1,0:T(8,128)(2,1)S(1)} %copy-done.1, ...), custom_call_target="tpu_custom_call", output_to_operand_aliasing={{0}: (4, {}), {1}: (5, {}), {2}: (6, {})} | custom-call | flops 1610612736 | bytes 8388608 | tf_op jit(solution)/shard_map/rubric_attention/pallas_call | solution.py:227
  51.4 2.4 %collective-permute-start.7 = (bf16[512,256]{1,0:T(8,128)(2,1)S(1)}, bf16[512,256]{1,0:T(8,128)(2,1)S(1)}, u32[]{:S(2)}, u32[]{:S(2)}) collective-permute-start(bf16[512,256]{1,0:T(8,128)(2,1)S(1)} %get-tuple-element.81), channel_id=1, source_target_pairs={{0,10},{2,8},{4,14},{6,12},{8,2},{10,0},{12,6},{14,4},{1,11},{3,9}... | collective-permute-start | bytes 786440 | tf_op jit(solution)/shard_map/ppermute | solution.py:388
  53.8 6.8 %response_attention.8 = (f32[4,2,8,128]{3,2,1,0:T(8,128)S(1)}, f32[4,2,144,2048]{3,2,1,0:T(8,128)S(1)}, bf16[4,256,2048]{2,1,0:T(8,128)(2,1)}) custom-call(s32[40]{0:T(128)S(1)} %copy-done.3, bf16[512,256]{1,0:T(8,128)(2,1)S(1)} %get-tuple-element.52.refs_0_.kv_ref, ...), custom_call_target="tpu_custom_call", output_to_operand_aliasing={{0}: (3, {}), {1}: (4, {})} | custom-call | flops 805306368 | bytes 6291456 | tf_op jit(solution)/shard_map/response_attention/pallas_call | solution.py:326
  60.7 6.7 %response_attention.9 = (f32[4,2,8,128]{3,2,1,0:T(8,128)S(1)}, f32[4,2,144,2048]{3,2,1,0:T(8,128)S(1)}, bf16[4,256,2048]{2,1,0:T(8,128)(2,1)}) custom-call(s32[40]{0:T(128)S(1)} %copy-done.3, bf16[512,256]{1,0:T(8,128)(2,1)S(1)} %collective-permute-done.3.kv_ref, ...), custom_call_target="tpu_custom_call", output_to_operand_aliasing={{0}: (3, {}), {1}: (4, {}), {2}: (5, {})} | custom-call | flops 805306368 | bytes 6291456 | tf_op jit(solution)/shard_map/response_attention/pallas_call | solution.py:326
  67.3 6.7 %response_attention.10 = (f32[4,2,8,128]{3,2,1,0:T(8,128)S(1)}, f32[4,2,144,2048]{3,2,1,0:T(8,128)S(1)}, bf16[4,256,2048]{2,1,0:T(8,128)(2,1)}) custom-call(s32[40]{0:T(128)S(1)} %copy-done.3, bf16[512,256]{1,0:T(8,128)(2,1)S(1)} %collective-permute-done.2.kv_ref, ...), custom_call_target="tpu_custom_call", output_to_operand_aliasing={{0}: (3, {}), {1}: (4, {}), {2}: (5, {})} | custom-call | flops 805306368 | bytes 6291456 | tf_op jit(solution)/shard_map/response_attention/pallas_call | solution.py:326
  74.0 6.7 %response_attention.11 = (f32[4,2,8,128]{3,2,1,0:T(8,128)S(1)}, f32[4,2,144,2048]{3,2,1,0:T(8,128)S(1)}, bf16[4,256,2048]{2,1,0:T(8,128)(2,1)}) custom-call(s32[40]{0:T(128)S(1)} %copy-done.3, bf16[512,256]{1,0:T(8,128)(2,1)S(1)} %collective-permute-done.1.kv_ref, ...), custom_call_target="tpu_custom_call", output_to_operand_aliasing={{0}: (3, {}), {1}: (4, {}), {2}: (5, {})} | custom-call | flops 805306368 | bytes 6291456 | tf_op jit(solution)/shard_map/response_attention/pallas_call | solution.py:326
  80.7 7.3 %response_attention.12 = (f32[4,2,8,128]{3,2,1,0:T(8,128)S(1)}, f32[4,2,144,2048]{3,2,1,0:T(8,128)S(1)}, bf16[4,256,2048]{2,1,0:T(8,128)(2,1)}) custom-call(s32[40]{0:T(128)S(1)} %copy-done.3, bf16[512,256]{1,0:T(8,128)(2,1)S(1)} %collective-permute-done.5.kv_ref, ...), custom_call_target="tpu_custom_call", output_to_operand_aliasing={{0}: (3, {}), {1}: (4, {}), {2}: (5, {})} | custom-call | flops 805306368 | bytes 6291456 | tf_op jit(solution)/shard_map/response_attention/pallas_call | solution.py:326
  88.0 0.9 collective-permute-start.6
  88.9 1.5 %collective-permute-start.4 = (bf16[512,256]{1,0:T(8,128)(2,1)S(1)}, bf16[512,256]{1,0:T(8,128)(2,1)S(1)}, u32[]{:S(2)}, u32[]{:S(2)}) collective-permute-start(bf16[512,256]{1,0:T(8,128)(2,1)S(1)} %get-tuple-element.72), channel_id=1, source_target_pairs={{0,8},{2,10},{4,12},{6,14},{8,0},{10,2},{12,4},{14,6},{1,9},{3,11}... | collective-permute-start | bytes 786440 | tf_op jit(solution)/shard_map/ppermute | solution.py:388
  90.4 7.1 %response_attention.13 = (f32[4,2,8,128]{3,2,1,0:T(8,128)S(1)}, f32[4,2,144,2048]{3,2,1,0:T(8,128)S(1)}, bf16[4,256,2048]{2,1,0:T(8,128)(2,1)}) custom-call(s32[40]{0:T(128)S(1)} %copy-done.3, bf16[512,256]{1,0:T(8,128)(2,1)S(1)} %collective-permute-done.7.kv_ref, ...), custom_call_target="tpu_custom_call", output_to_operand_aliasing={{0}: (3, {}), {1}: (4, {}), {2}: (5, {})} | custom-call | flops 805306368 | bytes 6291456 | tf_op jit(solution)/shard_map/response_attention/pallas_call | solution.py:326
  97.5 7.1 %response_attention.14 = (f32[4,2,8,128]{3,2,1,0:T(8,128)S(1)}, f32[4,2,144,2048]{3,2,1,0:T(8,128)S(1)}, bf16[4,256,2048]{2,1,0:T(8,128)(2,1)}) custom-call(s32[40]{0:T(128)S(1)} %copy-done.3, bf16[512,256]{1,0:T(8,128)(2,1)S(1)} %collective-permute-done.6.kv_ref, ...), custom_call_target="tpu_custom_call", output_to_operand_aliasing={{0}: (3, {}), {1}: (4, {}), {2}: (5, {})} | custom-call | flops 805306368 | bytes 6291456 | tf_op jit(solution)/shard_map/response_attention/pallas_call | solution.py:326
  104.6 7.1 %response_attention.15 = (f32[4,2,8,128]{3,2,1,0:T(8,128)S(1)}, f32[4,2,144,2048]{3,2,1,0:T(8,128)S(1)}, bf16[4,256,2048]{2,1,0:T(8,128)(2,1)}) custom-call(s32[40]{0:T(128)S(1)} %copy-done.3, bf16[512,256]{1,0:T(8,128)(2,1)S(1)} %collective-permute-done.4.kv_ref, ...), custom_call_target="tpu_custom_call", output_to_operand_aliasing={{0}: (3, {}), {1}: (4, {}), {2}: (5, {})} | custom-call | flops 805306368 | bytes 6291456 | tf_op jit(solution)/shard_map/response_attention/pallas_call | solution.py:326
  (18 shorter events, 0.0 us)
Async XLA Ops:
  9.4 10.4 %collective-permute-start = (f32[1024,512]{1,0:T(8,128)}, f32[1024,512]{1,0:T(8,128)S(1)}, u32[]{:S(2)}, u32[]{:S(2)}) collective-permute-start(f32[1024,512]{1,0:T(8,128)} %get-tuple-element.49), channel_id=1, source_target_pairs={{0,1},{1,0},{2,3},{3,2},{4,5},{5,4},{6,7},{7,6},{8,9},{9,8},{10,11... | collective-permute-start | bytes 6291464 | tf_op jit(solution)/shard_map/ppermute | solution.py:377
  9.9 6.5 %copy-start.4 = (bf16[4,256,4096]{2,1,0:T(8,128)(2,1)S(1)}, bf16[4,256,4096]{2,1,0:T(8,128)(2,1)}, u32[]{:S(2)}) copy-start(bf16[4,256,4096]{2,1,0:T(8,128)(2,1)} %param.13) | copy-start | bytes 25165828
  9.9 7.6 %copy-start.5 = (bf16[4096,512]{1,0:T(8,128)(2,1)S(1)}, bf16[4096,512]{1,0:T(8,128)(2,1)}, u32[]{:S(2)}) copy-start(bf16[4096,512]{1,0:T(8,128)(2,1)} %value_ref.1) | copy-start | bytes 12582916
  17.5 2.4 %copy-start.3 = (s32[40]{0:T(128)S(1)}, s32[40]{0:T(128)}, u32[]{:S(2)}) copy-start(s32[40]{0:T(128)} %get-tuple-element.48.plan_ref) | copy-start | bytes 484
  17.5 8.9 %copy-start.1 = (bf16[4,256,256]{2,1,0:T(8,128)(2,1)S(1)}, bf16[4,256,256]{2,1,0:T(8,128)(2,1)}, u32[]{:S(2)}) copy-start(bf16[4,256,256]{2,1,0:T(8,128)(2,1)} %k_ref.3) | copy-start | bytes 1572868
  17.5 8.9 %copy-start.2 = (bf16[4,256,256]{2,1,0:T(8,128)(2,1)S(1)}, bf16[4,256,256]{2,1,0:T(8,128)(2,1)}, u32[]{:S(2)}) copy-start(bf16[4,256,256]{2,1,0:T(8,128)(2,1)} %v_ref.3) | copy-start | bytes 1572868
  19.8 6.6 %copy-start = (bf16[4,256,2048]{2,1,0:T(8,128)(2,1)S(1)}, bf16[4,256,2048]{2,1,0:T(8,128)(2,1)}, u32[]{:S(2)}) copy-start(bf16[4,256,2048]{2,1,0:T(8,128)(2,1)} %q_ref.3) | copy-start | bytes 12582916
  20.8 53.2 %collective-permute-start.1 = (bf16[512,256]{1,0:T(8,128)(2,1)S(1)}, bf16[512,256]{1,0:T(8,128)(2,1)S(1)}, u32[]{:S(2)}, u32[]{:S(2)}) collective-permute-start(bf16[512,256]{1,0:T(8,128)(2,1)S(1)} %get-tuple-element.51), channel_id=1, source_target_pairs={{0,14},{2,12},{4,10},{6,8},{8,6},{10,4},{12,2},{14,0},{1,15},{3,13... | collective-permute-start | bytes 786440 | tf_op jit(solution)/shard_map/ppermute | solution.py:388
  26.4 25.0 %collective-permute-start.3 = (bf16[512,256]{1,0:T(8,128)(2,1)S(1)}, bf16[512,256]{1,0:T(8,128)(2,1)S(1)}, u32[]{:S(2)}, u32[]{:S(2)}) collective-permute-start(bf16[512,256]{1,0:T(8,128)(2,1)S(1)} %get-tuple-element.59), channel_id=1, source_target_pairs={{0,6},{2,4},{4,2},{6,0},{8,14},{10,12},{12,10},{14,8},{1,7},{3,5},... | collective-permute-start | bytes 786440 | tf_op jit(solution)/shard_map/ppermute | solution.py:388
  37.8 29.5 %collective-permute-start.2 = (bf16[512,256]{1,0:T(8,128)(2,1)S(1)}, bf16[512,256]{1,0:T(8,128)(2,1)S(1)}, u32[]{:S(2)}, u32[]{:S(2)}) collective-permute-start(bf16[512,256]{1,0:T(8,128)(2,1)S(1)} %get-tuple-element.58), channel_id=1, source_target_pairs={{0,4},{2,6},{4,0},{6,2},{8,12},{10,14},{12,8},{14,10},{1,5},{3,7},... | collective-permute-start | bytes 786440 | tf_op jit(solution)/shard_map/ppermute | solution.py:388
  39.9 40.8 %collective-permute-start.5 = (bf16[512,256]{1,0:T(8,128)(2,1)S(1)}, bf16[512,256]{1,0:T(8,128)(2,1)S(1)}, u32[]{:S(2)}, u32[]{:S(2)}) collective-permute-start(bf16[512,256]{1,0:T(8,128)(2,1)S(1)} %get-tuple-element.75), channel_id=1, source_target_pairs={{0,12},{2,14},{4,8},{6,10},{8,4},{10,6},{12,0},{14,2},{1,13},{3,15... | collective-permute-start | bytes 786440 | tf_op jit(solution)/shard_map/ppermute | solution.py:388
  51.4 39.1 %collective-permute-start.7 = (bf16[512,256]{1,0:T(8,128)(2,1)S(1)}, bf16[512,256]{1,0:T(8,128)(2,1)S(1)}, u32[]{:S(2)}, u32[]{:S(2)}) collective-permute-start(bf16[512,256]{1,0:T(8,128)(2,1)S(1)} %get-tuple-element.81), channel_id=1, source_target_pairs={{0,10},{2,8},{4,14},{6,12},{8,2},{10,0},{12,6},{14,4},{1,11},{3,9}... | collective-permute-start | bytes 786440 | tf_op jit(solution)/shard_map/ppermute | solution.py:388
  88.0 9.5 %collective-permute-start.6 = (bf16[512,256]{1,0:T(8,128)(2,1)S(1)}, bf16[512,256]{1,0:T(8,128)(2,1)S(1)}, u32[]{:S(2)}, u32[]{:S(2)}) collective-permute-start(bf16[512,256]{1,0:T(8,128)(2,1)S(1)} %get-tuple-element.79), channel_id=1, source_target_pairs={{0,2},{2,0},{4,6},{6,4},{8,10},{10,8},{12,14},{14,12},{1,3},{3,1},... | collective-permute-start | bytes 786440 | tf_op jit(solution)/shard_map/ppermute | solution.py:388
  88.9 15.7 %collective-permute-start.4 = (bf16[512,256]{1,0:T(8,128)(2,1)S(1)}, bf16[512,256]{1,0:T(8,128)(2,1)S(1)}, u32[]{:S(2)}, u32[]{:S(2)}) collective-permute-start(bf16[512,256]{1,0:T(8,128)(2,1)S(1)} %get-tuple-element.72), channel_id=1, source_target_pairs={{0,8},{2,10},{4,12},{6,14},{8,0},{10,2},{12,4},{14,6},{1,9},{3,11}... | collective-permute-start | bytes 786440 | tf_op jit(solution)/shard_map/ppermute | solution.py:388
